TPU v7x, 32 devices: a whole 2x2x4 slice. The times are simulated.
32 devices in a mesh: blk: 8 (over y, x, core), rep: 4 (over z).
Axes of the slice: x: 2, y: 2, z: 4, core: 2. Of those that a mesh axis runs over, the one named last changes fastest.
Arguments:
- features: bfloat16 [8192, 128], P(('blk', 'rep')), may hold values from -6 to 6
- node_degree: int32 [8192], P(('blk', 'rep')), may hold values from 1 to 16
- edge_target: int32 [8, 4, 768], P('blk', 'rep'), may hold values from 0 to 1023
- edge_source: int32 [8, 4, 768], P('blk', 'rep'), may hold values from 0 to 255
- edge_count: int32 [8, 4, 8], P('blk', 'rep'), may hold values from 0 to 96, as said below
- layer_weight: bfloat16 [128, 256], replicated, may hold values from -0.5 to 0.5
- layer_bias: float32 [256], replicated, may hold values from -3 to 3
- cotangent: bfloat16 [8192, 256], P(('blk', 'rep')), may hold values from -0.06591797 to 0.06591797
Outputs:
- hidden: bfloat16 [8192, 256], P(('blk', 'rep'))
- grad_weight: float32 [128, 256], replicated
- grad_bias: float32 [256], replicated
Inputs may be any that keep to these rules, and one draw needn't show every extreme that they name: edge_count[b, q, c] is at most 96, and edge_count[b, q, b] equals 96 for every b and q.
All inputs are finite; a program needn't handle non-finite values.
Results may differ from a plain program's by a relative error of at most 0.0058.
Values may be sent and summed in bfloat16 or wider, within the bound.
A program may use at most 64 MiB of HBM per device.

v0:
```python
import jax
import jax.numpy as jnp
from jax import lax
from jax.sharding import PartitionSpec as P


def per_device(
    features, node_degree, edge_target, edge_source, edge_count, layer_weight, layer_bias, cotangent
):
    quarter = features.shape[0]
    width = features.shape[1]
    blocks = lax.axis_size("blk")
    slots = edge_target.shape[-1]
    per_block = slots // blocks
    row_count = quarter * lax.axis_size("rep")
    inv_root = lax.rsqrt(node_degree.astype(jnp.float32))
    scaled = (features.astype(jnp.float32) * inv_root[:, None]).astype(jnp.bfloat16)
    targets = edge_target.reshape(slots)
    sources = edge_source.reshape(slots)
    counts = edge_count.reshape(blocks)
    live = (jnp.arange(per_block, dtype=jnp.int32)[None, :] < counts[:, None]).reshape(slots)
    slot_block = jnp.arange(slots, dtype=jnp.int32) // per_block
    source_index = slot_block * quarter + sources
    empty = jnp.zeros((row_count, width), jnp.float32)
    piece = lax.all_gather(scaled, "blk", axis=0, tiled=True)
    length = piece.shape[0]
    usable = live & (source_index >= 0) & (source_index < length)
    rows = piece[jnp.clip(source_index, 0, length - 1)].astype(jnp.float32) * usable[
        :, None
    ].astype(jnp.float32)
    partial_value = empty.at[targets].add(rows)
    total = lax.psum(partial_value, "rep")
    own_rows = lax.dynamic_slice_in_dim(total, lax.axis_index("rep") * quarter, quarter, 0)
    aggregated = (inv_root[:, None] * (own_rows + scaled.astype(jnp.float32))).astype(jnp.bfloat16)
    pre = jnp.dot(aggregated, layer_weight, preferred_element_type=jnp.float32) + layer_bias
    hidden = jax.nn.silu(pre).astype(jnp.bfloat16)
    sig = jax.nn.sigmoid(pre)
    grad_pre = cotangent.astype(jnp.float32) * sig * (1.0 + pre * (1.0 - sig))
    grad_pre_b = grad_pre.astype(jnp.bfloat16)
    local_weight = jnp.einsum(
        "nf,nh->fh", aggregated, grad_pre_b, preferred_element_type=jnp.float32
    )
    local_bias = jnp.sum(grad_pre, axis=0)
    grad_weight, grad_bias = lax.psum((local_weight, local_bias), ("blk", "rep"))
    return (hidden, grad_weight, grad_bias)


def solution(mesh):
    in_specs = (
        P(("blk", "rep"), None),
        P(("blk", "rep")),
        P("blk", "rep", None),
        P("blk", "rep", None),
        P("blk", "rep", None),
        P(),
        P(),
        P(("blk", "rep"), None),
    )
    out_specs = (P(("blk", "rep"), None), P(), P())
    return jax.shard_map(
        per_device, mesh=mesh, in_specs=in_specs, out_specs=out_specs, check_vma=False
    )
```

profile of v0, /device:TPU:0, one launch (start us, length us, event | category | flops | bytes accessed | tf_op | source)
XLA Modules:
  0.0 207.8 jit_solution(2491169909878290600)
XLA Ops:
  7.2 0.0 copy-start
  7.2 0.0 all-reduce.3.cloned.1.call-start
  7.2 0.0 copy-start.6
  7.2 0.7 fusion.12
  7.9 0.0 copy-start.2
  8.0 0.0 copy-done.6
  8.0 0.1 iota_compare_fusion
  8.0 0.1 lt.59
  8.1 0.5 copy-done.2
  8.7 0.0 copy-start.3
  8.7 0.6 copy-done.3
  9.3 0.9 multiply_convert_fusion.2
  10.3 11.3 %all_gather.3 = bf16[2048,128]{1,0:T(8,128)(2,1)S(1)} all-gather(bf16[256,128]{1,0:T(8,128)(2,1)S(1)} %multiply_convert_fusion.2), channel_id=1, replica_groups=mesh['blk'=8,'rep'=4] {'blk'}, dimensions={0}, use_global_device_ids=true | all-gather | bytes 589824 | tf_op jit(solution)/shard_map/all_gather | solution.py:25
  21.6 10.4 %scatter_custom_fusion = f32[1024,128]{1,0:T(8,128)} fusion(s32[768]{0:T(1024)S(1)} %fusion.12, f32[]{:T(128)} %constant.11.clone.1, f32[768]{0:T(1024)S(1)} %and_convert_fusion, bf16[2048,128]{1,0:T(8,128)(2,1)S(1)} %all_gather.3, s32[1024]{0:T(1024)S(1)} %pad_clamp_fusion), kind=kCustom, calls=%fused_computation.3 | custom fusion | flops 294912 | bytes 1056772 | tf_op jit(solution)/shard_map/scatter-add | solution.py:31
  32.0 0.0 copy-start.1
  32.0 0.0 all-reduce.3.cloned.1.call-update
  32.0 0.0 all-reduce.5.cloned.1.call-start
  32.1 0.0 copy-start.4
  32.1 0.0 copy-start.5
  32.1 38.7 %all-reduce.3.cloned.1.call-done = f32[1024,128]{1,0:T(8,128)} async-done(((f32[1024,128]{1,0:T(8,128)}), f32[1024,128]{1,0:T(8,128)}) %all-reduce.3.cloned.1.call-update) | async-done | bytes 524304 | tf_op jit(solution)/shard_map/psum | solution.py:32
  70.8 0.0 copy-done.1
  70.8 1.0 multiply_convert_fusion.1
  71.8 0.0 copy-done
  71.8 0.0 copy-done.4
  71.8 0.0 copy-done.5
  71.8 0.9 fusion.18
  72.8 0.9 fusion.5
  73.6 0.0 all-reduce.5.cloned.1.call-update
  73.6 40.0 %psum.23 = f32[256]{0:T(256)} all-reduce(f32[256]{0:T(256)S(1)} %get-tuple-element.3), channel_id=1, replica_groups=mesh['blk'=8,'rep'=4] {'blk','rep'}, use_global_device_ids=true, to_apply=%region_4.5 | all-reduce | flops 256 | bytes 2048 | tf_op jit(solution)/shard_map/psum | solution.py:44
  113.6 85.8 %all-reduce.5.cloned.1.call-done = f32[128,256]{1,0:T(8,128)} async-done(((f32[128,256]{1,0:T(8,128)}), f32[128,256]{1,0:T(8,128)}) %all-reduce.5.cloned.1.call-update) | async-done | bytes 131088 | tf_op jit(solution)/shard_map/psum | solution.py:44
  199.4 1.6 copy.13
  (5 shorter events, 0.1 us)
Async XLA Ops:
  7.2 64.6 %copy-start = (bf16[128,256]{1,0:T(8,128)(2,1)S(1)}, bf16[128,256]{1,0:T(8,128)(2,1)}, u32[]{:S(2)}) copy-start(bf16[128,256]{1,0:T(8,128)(2,1)} %param.13) | copy-start | bytes 196612
  7.2 63.6 %all-reduce.3.cloned.1.call-start = ((), (), s32[]{:S(2)}) async-start(), calls=%async_computation | async-start | bytes 1048576 | tf_op jit(solution)/shard_map/psum | solution.py:32
  7.2 0.7 copy-start.6
  7.9 0.7 copy-start.2
  8.7 0.7 copy-start.3
  32.0 38.8 %copy-start.1 = (bf16[256,128]{1,0:T(8,128)(2,1)S(1)}, bf16[256,128]{1,0:T(8,128)(2,1)}, u32[]{:S(2)}) copy-start(bf16[256,128]{1,0:T(8,128)(2,1)} %param.8) | copy-start | bytes 196612
  32.0 167.4 %all-reduce.5.cloned.1.call-start = ((), (), s32[]{:S(2)}) async-start(), calls=%async_computation.1 | async-start | bytes 262144 | tf_op jit(solution)/shard_map/psum | solution.py:44
  32.1 39.7 %copy-start.4 = (bf16[256,256]{1,0:T(8,128)(2,1)S(1)}, bf16[256,256]{1,0:T(8,128)(2,1)}, u32[]{:S(2)}) copy-start(bf16[256,256]{1,0:T(8,128)(2,1)} %param.15) | copy-start | bytes 393220
  32.1 39.7 %copy-start.5 = (f32[256]{0:T(256)S(1)}, f32[256]{0:T(256)}, u32[]{:S(2)}) copy-start(f32[256]{0:T(256)} %param.14) | copy-start | bytes 3076
Sparse Core Ops, SparseCore 0:
  32.2 38.5 all-reduce.2
  76.9 122.4 all-reduce.4
where the time goes:
time: 208 us
  waiting for transfers between devices  125 us (60%)
  blocking collectives  51.3 us (25%)
  between operations  14.2 us (7%)
  other arithmetic  13.2 us (6%)
  local copies, waits for them, and re-layouts  2.84 us (1%)
    psum x1, waiting for transfers between devices, per_device(): lax.psum((local_weight, local_bias), ('blk', 'rep'))  85.8 us
    psum x1, blocking collectives, per_device(): lax.psum((local_weight, local_bias), ('blk', 'rep'))  40 us
    psum x1, waiting for transfers between devices, per_device(): total = lax.psum(partial_value, 'rep')  38.7 us
    all_gather x1, blocking collectives, per_device(): piece = lax.all_gather(scaled, 'blk', axis=0, tiled=True)  11.3 us
    scatter-add x1, other arithmetic, per_device(): partial_value = empty.at[targets].add(rows)  10.4 us
  transfers between devices with their start and end apart: 2, of which 2 were waited for; matrix products, arithmetic and copies ran while one was open for 0% of the time, Pallas kernels for 0%

commit v1 on v0

--- a/solution.py
+++ b/solution.py
@@ -1,7 +1,216 @@
+import functools
+
 import jax
 import jax.numpy as jnp
 from jax import lax
+from jax.experimental import pallas as pl
+from jax.experimental.pallas import tpu as pltpu
 from jax.sharding import PartitionSpec as P
+
+MESH = pl.DeviceIdType.MESH
+LANES = 128
+
+
+def layer_kernel(
+    feat, deg, tgt, src, cnt, w, bias, cot,
+    hid, gw, gb,
+    ag, onehot, pick, gt, rs_out, rs_in, g_out, g_in, z_buf, f_buf,
+    ag_s, ag_r, rs_s, rs_r, g_s, g_r, z_s, z_r, f_s, f_r,
+):
+    f32, bf16 = jnp.float32, jnp.bfloat16
+    b, q = lax.axis_index("blk"), lax.axis_index("rep")
+    blocks, reps = ag.shape[0], z_buf.shape[0]
+    quarter, width = feat.shape
+    per_block = tgt.shape[-1] // blocks
+    core, x, y = lax.rem(b, 2), lax.rem(lax.div(b, 2), 2), lax.div(b, 4)
+
+    def peer(k):
+        return (
+            lax.rem(core + k % 2, 2)
+            + 2 * lax.rem(x + (k // 2) % 2, 2)
+            + 4 * lax.rem(y + k // 4, 2)
+        )
+
+    def up(k):
+        return lax.rem(q + k, reps)
+
+    def push(source, target, send, recv, to_b, to_q):
+        return pltpu.make_async_remote_copy(
+            src_ref=source, dst_ref=target, send_sem=send, recv_sem=recv,
+            device_id=(to_b, to_q), device_id_type=MESH,
+        )
+
+    barrier = pltpu.get_barrier_semaphore()
+    for k in range(1, blocks):
+        pl.semaphore_signal(barrier, inc=1, device_id=(peer(k), q), device_id_type=MESH)
+    for k in range(1, reps):
+        pl.semaphore_signal(barrier, inc=1, device_id=(b, up(k)), device_id_type=MESH)
+
+    inv_row = lax.rsqrt(deg[...].astype(f32))
+    ag[b] = (feat[...].astype(f32).T * inv_row).astype(bf16)
+
+    pl.semaphore_wait(barrier, blocks + reps - 2)
+
+    sends = []
+    for k in (6, 2, 4, 1):
+        copy = push(ag.at[b], ag.at[b], ag_s.at[k], ag_r.at[b], peer(k), q)
+        copy.start()
+        sends.append(copy)
+
+    def arrived(k):
+        p = peer(k)
+        push(ag.at[p], ag.at[p], ag_s.at[k], ag_r.at[p], peer(k), q).wait_recv()
+
+    eye = lax.broadcasted_iota(jnp.int32, (quarter, quarter), 0) == lax.broadcasted_iota(
+        jnp.int32, (quarter, quarter), 1
+    )
+    inv = jnp.sum(jnp.where(eye, inv_row, 0.0), axis=1, keepdims=True)
+    scaled = (feat[...].astype(f32) * inv).astype(bf16).astype(f32)
+
+    node = lax.broadcasted_iota(jnp.int32, (quarter, LANES), 0)
+    lane = lax.broadcasted_iota(jnp.int32, (1, LANES), 1)
+    fill = jnp.full((1, LANES - per_block), -1, jnp.int32)
+    for c in range(blocks):
+        here = pl.ds(c * LANES, LANES)
+        live = lane < cnt[0, :, c : c + 1]
+        s_c = jnp.concatenate([src[0, :, c * per_block : (c + 1) * per_block], fill], axis=1)
+        t_c = jnp.concatenate([tgt[0, :, c * per_block : (c + 1) * per_block], fill], axis=1)
+        t_c = jnp.where(live, t_c, -1)
+        pick[c] = jnp.where(node == s_c, 1.0, 0.0).astype(bf16)
+        for k in range(reps):
+            onehot[k, :, here] = jnp.where(node + up(k) * quarter == t_c, 1.0, 0.0).astype(bf16)
+
+    for k in (2, 4, 6):
+        arrived(k)
+        p = peer(k)
+        copy = push(ag.at[p], ag.at[p], ag_s.at[k + 1], ag_r.at[p], peer(1), q)
+        copy.start()
+        sends.append(copy)
+    for k in (1, 3, 5, 7):
+        arrived(k)
+
+    for c in range(blocks):
+        rows = jnp.dot(ag[c], pick[c], preferred_element_type=f32)
+        gt[:, pl.ds(c * LANES, LANES)] = rows.astype(bf16)
+
+    own = None
+    for k in (2, 1, 3, 0):
+        part = lax.dot_general(
+            onehot[k], gt[...], (((1,), (1,)), ((), ())), preferred_element_type=f32
+        )
+        if k:
+            rs_out[k - 1] = part.astype(bf16)
+            copy = push(
+                rs_out.at[k - 1], rs_in.at[k - 1], rs_s.at[k - 1], rs_r.at[k - 1], b, up(k)
+            )
+            copy.start()
+            sends.append(copy)
+        else:
+            own = part + scaled
+    for k in (1, 3, 2):
+        push(
+            rs_out.at[k - 1], rs_in.at[k - 1], rs_s.at[k - 1], rs_r.at[k - 1], b, up(k)
+        ).wait_recv()
+        own = own + rs_in[k - 1].astype(f32)
+
+    agg = (own * inv).astype(bf16)
+    pre = jnp.dot(agg, w[...], preferred_element_type=f32) + bias[...]
+    sig = 1.0 / (1.0 + jnp.exp(-pre))
+    grad = cot[...].astype(f32) * sig * (1.0 + pre * (1.0 - sig))
+    gwl = lax.dot_general(
+        agg, grad.astype(bf16), (((0,), (0,)), ((), ())), preferred_element_type=f32
+    )
+    gbl = jnp.sum(grad, axis=0, keepdims=True)
+    step = width // blocks
+    hw = gw.shape[1]
+    row = lax.broadcasted_iota(jnp.int32, (step, LANES), 0)
+    extra = jnp.where(row == 0, gbl[:, :LANES], jnp.where(row == 1, gbl[:, LANES:], 0.0))
+    for j in range(blocks):
+        g_out[j, :, :hw] = gwl[j * step : (j + 1) * step].astype(bf16)
+        g_out[j, :, hw:] = extra.astype(bf16)
+
+    def share(k):
+        return push(g_out.at[peer(k)], g_in.at[k - 1], g_s.at[k - 1], g_r.at[k - 1], peer(k), q)
+
+    for k in (6, 7, 2, 3, 4, 5, 1):
+        copy = share(k)
+        copy.start()
+        sends.append(copy)
+    hid[...] = (pre * sig).astype(bf16)
+    part = g_out[b].astype(f32)
+    for k in (1, 2, 3, 4, 5, 6, 7):
+        share(k).wait_recv()
+        part = part + g_in[k - 1].astype(f32)
+    z_buf[q] = part.astype(bf16)
+    for k in (2, 1, 3):
+        copy = push(z_buf.at[q], z_buf.at[q], z_s.at[k], z_r.at[q], b, up(k))
+        copy.start()
+        sends.append(copy)
+    for k in (1, 3, 2):
+        p = up(k)
+        push(z_buf.at[p], z_buf.at[p], z_s.at[k], z_r.at[p], b, p).wait_recv()
+    part = z_buf[0].astype(f32)
+    for k in range(1, reps):
+        part = part + z_buf[k].astype(f32)
+    f_buf[b] = part.astype(bf16)
+    for k in (6, 7, 2, 3, 4, 5, 1):
+        copy = push(f_buf.at[b], f_buf.at[b], f_s.at[k], f_r.at[b], peer(k), q)
+        copy.start()
+        sends.append(copy)
+    for k in (1, 2, 3, 4, 5, 6, 7):
+        p = peer(k)
+        push(f_buf.at[p], f_buf.at[p], f_s.at[k], f_r.at[p], p, q).wait_recv()
+    for j in range(blocks):
+        gw[j * step : (j + 1) * step, :] = f_buf[j, :, :hw].astype(f32)
+    gb[:, :LANES] = f_buf[0, 0:1, hw : hw + LANES].astype(f32)
+    gb[:, LANES:] = f_buf[0, 1:2, hw : hw + LANES].astype(f32)
+    for copy in sends:
+        copy.wait_send()
+
+
+def fused_per_device(
+    features, node_degree, edge_target, edge_source, edge_count, layer_weight, layer_bias, cotangent
+):
+    quarter, width = features.shape
+    blocks, reps = lax.axis_size("blk"), lax.axis_size("rep")
+    hw = layer_weight.shape[1]
+    step = width // blocks
+    bf16 = jnp.bfloat16
+    dma = pltpu.SemaphoreType.DMA
+    hidden, grad_weight, grad_bias = pl.pallas_call(
+        layer_kernel,
+        out_shape=(
+            jax.ShapeDtypeStruct((quarter, hw), bf16),
+            jax.ShapeDtypeStruct((width, hw), jnp.float32),
+            jax.ShapeDtypeStruct((1, hw), jnp.float32),
+        ),
+        in_specs=[pl.BlockSpec(memory_space=pltpu.VMEM)] * 8,
+        out_specs=[pl.BlockSpec(memory_space=pltpu.VMEM)] * 3,
+        scratch_shapes=[
+            pltpu.VMEM((blocks, width, quarter), bf16),
+            pltpu.VMEM((reps, quarter, blocks * LANES), bf16),
+            pltpu.VMEM((blocks, quarter, LANES), bf16),
+            pltpu.VMEM((width, blocks * LANES), bf16),
+            pltpu.VMEM((reps - 1, quarter, width), bf16),
+            pltpu.VMEM((reps - 1, quarter, width), bf16),
+            pltpu.VMEM((blocks, step, hw + LANES), bf16),
+            pltpu.VMEM((blocks - 1, step, hw + LANES), bf16),
+            pltpu.VMEM((reps, step, hw + LANES), bf16),
+            pltpu.VMEM((blocks, step, hw + LANES), bf16),
+            dma((blocks,)), dma((blocks,)),
+            dma((reps - 1,)), dma((reps - 1,)),
+            dma((blocks - 1,)), dma((blocks - 1,)),
+            dma((reps,)), dma((reps,)),
+            dma((blocks,)), dma((blocks,)),
+        ],
+        compiler_params=pltpu.CompilerParams(
+            collective_id=0, has_side_effects=True, vmem_limit_bytes=24 * 2**20
+        ),
+    )(
+        features, node_degree.reshape(1, quarter), edge_target, edge_source, edge_count,
+        layer_weight, layer_bias.reshape(1, hw), cotangent,
+    )
+    return hidden, grad_weight, grad_bias.reshape(hw)
 
 
 def per_device(
@@ -57,6 +266,7 @@
         P(("blk", "rep"), None),
     )
     out_specs = (P(("blk", "rep"), None), P(), P())
+    fused = mesh.shape["blk"] == 8 and mesh.shape["rep"] == 4
     return jax.shard_map(
-        per_device, mesh=mesh, in_specs=in_specs, out_specs=out_specs, check_vma=False
-    )
+        fused_per_device if fused else per_device, mesh=mesh, in_specs=in_specs, out_specs=out_specs, check_vma=False
+    )

time: 208 us -> 38 us (0.18)
  waiting for transfers between devices: 125 us -> 0 us
  blocking collectives: 51.3 us -> 0 us
  Pallas kernels: 0 us -> 29.8 us
  between operations: 14.2 us -> 0.67 us
  other arithmetic: 13.2 us -> 0 us
  local copies, waits for them, and re-layouts: 2.84 us -> 7.17 us
    psum x2 -> x0, waiting for transfers between devices: 124 us -> none  [the longest x1 85.8 us: per_device(): lax.psum((local_weight, local_bias), ('blk', 'rep'))]
    psum x1 -> x0, blocking collectives: 40 us -> none  [per_device(): lax.psum((local_weight, local_bias), ('blk', 'rep'))]
    pallas_call x0 -> x1, Pallas kernels: none -> 29.8 us  [fused_per_device(): pl.pallas_call(layer_kernel, out_shape=(jax.ShapeDtypeStruct((quarter, hw...]
    all_gather x1 -> x0, blocking collectives: 11.3 us -> none  [per_device(): piece = lax.all_gather(scaled, 'blk', axis=0, tiled=True)]
    scatter-add x1 -> x0, other arithmetic: 10.4 us -> none  [per_device(): partial_value = empty.at[targets].add(rows)]
    unnamed x15 -> x19, local copies, waits for them, and re-layouts: 2.76 us -> 7.17 us
  transfers between devices with their start and end apart: 2 -> 0, of which waited for: 2 -> 0; matrix products, arithmetic and copies ran while one was open for 0% -> 0% of each run, Pallas kernels for 0% -> 0%
where the time goes in v1:
time: 38 us; the launch traced here: 37.7 us
  Pallas kernels  29.8 us (78%)
  local copies, waits for them, and re-layouts  7.17 us (19%)
  between operations  0.67 us (2%)
    pallas_call x1, Pallas kernels, fused_per_device(): pl.pallas_call(layer_kernel, out_shape=(jax.ShapeDtypeStruct((quarter, hw...  29.8 us
    unnamed x19, local copies, waits for them, and re-layouts  7.17 us

profile of v1, /device:TPU:0, one launch (start us, length us, event | category | flops | bytes accessed | tf_op | source)
XLA Modules:
  0.0 37.7 jit_solution(12711465874734243277)
XLA Ops:
  0.6 0.0 copy-start.3
  0.6 0.0 copy-start.7
  0.7 0.7 %copy-done.3 = s32[1,1,768]{2,1,0:T(1,128)S(1)} copy-done((s32[1,1,768]{2,1,0:T(1,128)S(1)}, s32[1,1,768]{2,1,0:T(1,128)}, u32[]{:S(2)}) %copy-start.3) | copy-done | bytes 3096
  1.3 0.0 copy-done.7
  1.3 0.0 copy-start
  1.3 0.9 %copy-done = bf16[256,256]{1,0:T(8,128)(2,1)S(1)} copy-done((bf16[256,256]{1,0:T(8,128)(2,1)S(1)}, bf16[256,256]{1,0:T(8,128)(2,1)}, u32[]{:S(2)}) %copy-start) | copy-done | bytes 131096
  2.2 0.0 copy-start.1
  2.2 0.8 %copy-done.1 = bf16[256,128]{1,0:T(8,128)(2,1)S(1)} copy-done((bf16[256,128]{1,0:T(8,128)(2,1)S(1)}, bf16[256,128]{1,0:T(8,128)(2,1)}, u32[]{:S(2)}) %copy-start.1) | copy-done | bytes 65560
  3.1 0.0 copy-start.2
  3.1 0.8 %copy-done.2 = bf16[128,256]{1,0:T(8,128)(2,1)S(1)} copy-done((bf16[128,256]{1,0:T(8,128)(2,1)S(1)}, bf16[128,256]{1,0:T(8,128)(2,1)}, u32[]{:S(2)}) %copy-start.2) | copy-done | bytes 65560
  3.9 0.0 copy-start.4
  3.9 0.7 %copy-done.4 = s32[1,1,768]{2,1,0:T(1,128)S(1)} copy-done((s32[1,1,768]{2,1,0:T(1,128)S(1)}, s32[1,1,768]{2,1,0:T(1,128)}, u32[]{:S(2)}) %copy-start.4) | copy-done | bytes 3096
  4.6 0.0 copy-start.5
  4.6 0.7 %copy-done.5 = s32[256]{0:T(256)S(1)} copy-done((s32[256]{0:T(256)S(1)}, s32[256]{0:T(256)}, u32[]{:S(2)}) %copy-start.5) | copy-done | bytes 1048
  5.3 0.0 copy-start.6
  5.3 0.7 %copy-done.6 = f32[256]{0:T(256)S(1)} copy-done((f32[256]{0:T(256)S(1)}, f32[256]{0:T(256)}, u32[]{:S(2)}) %copy-start.6) | copy-done | bytes 1048
  6.0 29.8 %shard_map.103 = (bf16[256,256]{1,0:T(8,128)(2,1)S(1)}, f32[128,256]{1,0:T(8,128)S(1)}, f32[1,256]{1,0:T(1,128)S(1)}) custom-call(bf16[256,128]{1,0:T(8,128)(2,1)S(1)} %copy-done.1, s32[1,256]{1,0:T(1,128)S(1)} %bitcast.3, s32[1,1,768]{2,1,0:T(1,128)S(1)} %copy-done.3, s32[1,1,768]{2,1,0:T(1,128)S(1)} %copy-done.4, s32[1,1,8]{2,1,0:T(1,128)S(1)} %copy-done.7, ...), custom_call_target="tpu_custom_call" | custom-call | tf_op jit(solution)/shard_map/pallas_call | solution.py:180
  35.8 0.7 %copy.14 = bf16[256,256]{1,0:T(8,128)(2,1)} copy(bf16[256,256]{1,0:T(8,128)(2,1)S(1)} %get-tuple-element.12) | data formatting | bytes 262144
  36.4 0.7 %copy.15 = f32[128,256]{1,0:T(8,128)} copy(f32[128,256]{1,0:T(8,128)S(1)} %get-tuple-element.13) | data formatting | bytes 262144
  37.1 0.6 %copy.16 = f32[256]{0:T(256)} copy(f32[256]{0:T(256)S(1)} %bitcast.5) | data formatting | bytes 2048
Async XLA Ops:
  0.6 0.7 %copy-start.3 = (s32[1,1,768]{2,1,0:T(1,128)S(1)}, s32[1,1,768]{2,1,0:T(1,128)}, u32[]{:S(2)}) copy-start(s32[1,1,768]{2,1,0:T(1,128)} %tgt.1) | copy-start | bytes 9220
  0.6 0.7 %copy-start.7 = (s32[1,1,8]{2,1,0:T(1,128)S(1)}, s32[1,1,8]{2,1,0:T(1,128)}, u32[]{:S(2)}) copy-start(s32[1,1,8]{2,1,0:T(1,128)} %cnt.1) | copy-start | bytes 100
  1.3 0.9 %copy-start = (bf16[256,256]{1,0:T(8,128)(2,1)S(1)}, bf16[256,256]{1,0:T(8,128)(2,1)}, u32[]{:S(2)}) copy-start(bf16[256,256]{1,0:T(8,128)(2,1)} %cot.1) | copy-start | bytes 393220
  2.2 0.8 %copy-start.1 = (bf16[256,128]{1,0:T(8,128)(2,1)S(1)}, bf16[256,128]{1,0:T(8,128)(2,1)}, u32[]{:S(2)}) copy-start(bf16[256,128]{1,0:T(8,128)(2,1)} %feat.1) | copy-start | bytes 196612
  3.1 0.8 %copy-start.2 = (bf16[128,256]{1,0:T(8,128)(2,1)S(1)}, bf16[128,256]{1,0:T(8,128)(2,1)}, u32[]{:S(2)}) copy-start(bf16[128,256]{1,0:T(8,128)(2,1)} %w.1) | copy-start | bytes 196612
  3.9 0.7 %copy-start.4 = (s32[1,1,768]{2,1,0:T(1,128)S(1)}, s32[1,1,768]{2,1,0:T(1,128)}, u32[]{:S(2)}) copy-start(s32[1,1,768]{2,1,0:T(1,128)} %src.1) | copy-start | bytes 9220
  4.6 0.7 %copy-start.5 = (s32[256]{0:T(256)S(1)}, s32[256]{0:T(256)}, u32[]{:S(2)}) copy-start(s32[256]{0:T(256)} %param.9) | copy-start | bytes 3076
  5.3 0.7 %copy-start.6 = (f32[256]{0:T(256)S(1)}, f32[256]{0:T(256)}, u32[]{:S(2)}) copy-start(f32[256]{0:T(256)} %param.14) | copy-start | bytes 3076

commit v2 on v1

--- a/solution.py
+++ b/solution.py
@@ -12,10 +12,10 @@
 
 
 def layer_kernel(
-    feat, deg, tgt, src, cnt, w, bias, cot,
+    feat_h, deg_h, tgt_h, src_h, cnt_h, w_h, bias_h, cot_h,
     hid, gw, gb,
-    ag, onehot, pick, gt, rs_out, rs_in, g_out, g_in, z_buf, f_buf,
-    ag_s, ag_r, rs_s, rs_r, g_s, g_r, z_s, z_r, f_s, f_r,
+    feat, deg, tgt, src, cnt, w, bias, cot, ag, onehot, pick, gt, rs_out, rs_in, g_out, g_in, z_buf, f_buf,
+    in_s, ag_s, ag_r, rs_s, rs_r, g_s, g_r, z_s, z_r, f_s, f_r,
 ):
     f32, bf16 = jnp.float32, jnp.bfloat16
     b, q = lax.axis_index("blk"), lax.axis_index("rep")
@@ -40,12 +40,24 @@
             device_id=(to_b, to_q), device_id_type=MESH,
         )
 
+    loads = [
+        pltpu.make_async_copy(source, target, in_s.at[i])
+        for i, (source, target) in enumerate((
+            (feat_h, feat), (deg_h, deg), (tgt_h, tgt), (src_h, src),
+            (cnt_h, cnt), (w_h, w), (bias_h, bias), (cot_h, cot),
+        ))
+    ]
+    for load in loads:
+        load.start()
+
     barrier = pltpu.get_barrier_semaphore()
     for k in range(1, blocks):
         pl.semaphore_signal(barrier, inc=1, device_id=(peer(k), q), device_id_type=MESH)
     for k in range(1, reps):
         pl.semaphore_signal(barrier, inc=1, device_id=(b, up(k)), device_id_type=MESH)
 
+    loads[0].wait()
+    loads[1].wait()
     inv_row = lax.rsqrt(deg[...].astype(f32))
     ag[b] = (feat[...].astype(f32).T * inv_row).astype(bf16)
 
@@ -67,6 +79,8 @@
     inv = jnp.sum(jnp.where(eye, inv_row, 0.0), axis=1, keepdims=True)
     scaled = (feat[...].astype(f32) * inv).astype(bf16).astype(f32)
 
+    for load in loads[2:]:
+        load.wait()
     node = lax.broadcasted_iota(jnp.int32, (quarter, LANES), 0)
     lane = lax.broadcasted_iota(jnp.int32, (1, LANES), 1)
     fill = jnp.full((1, LANES - per_block), -1, jnp.int32)
@@ -168,6 +182,17 @@
         copy.wait_send()
 
 
+def write_kernel(hid, gw, gb, hid_h, gw_h, gb_h, sems):
+    copies = [
+        pltpu.make_async_copy(source, target, sems.at[i])
+        for i, (source, target) in enumerate(((hid, hid_h), (gw, gw_h), (gb, gb_h)))
+    ]
+    for copy in copies:
+        copy.start()
+    for copy in copies:
+        copy.wait()
+
+
 def fused_per_device(
     features, node_degree, edge_target, edge_source, edge_count, layer_weight, layer_bias, cotangent
 ):
@@ -177,6 +202,9 @@
     step = width // blocks
     bf16 = jnp.bfloat16
     dma = pltpu.SemaphoreType.DMA
+    def hbm(array):
+        return pltpu.with_memory_space_constraint(array, pltpu.HBM)
+
     hidden, grad_weight, grad_bias = pl.pallas_call(
         layer_kernel,
         out_shape=(
@@ -184,9 +212,17 @@
             jax.ShapeDtypeStruct((width, hw), jnp.float32),
             jax.ShapeDtypeStruct((1, hw), jnp.float32),
         ),
-        in_specs=[pl.BlockSpec(memory_space=pltpu.VMEM)] * 8,
+        in_specs=[pl.BlockSpec(memory_space=pltpu.HBM)] * 8,
         out_specs=[pl.BlockSpec(memory_space=pltpu.VMEM)] * 3,
         scratch_shapes=[
+            pltpu.VMEM((quarter, width), bf16),
+            pltpu.VMEM((1, quarter), jnp.int32),
+            pltpu.VMEM(edge_target.shape, jnp.int32),
+            pltpu.VMEM(edge_source.shape, jnp.int32),
+            pltpu.VMEM(edge_count.shape, jnp.int32),
+            pltpu.VMEM((width, hw), bf16),
+            pltpu.VMEM((1, hw), jnp.float32),
+            pltpu.VMEM((quarter, hw), bf16),
             pltpu.VMEM((blocks, width, quarter), bf16),
             pltpu.VMEM((reps, quarter, blocks * LANES), bf16),
             pltpu.VMEM((blocks, quarter, LANES), bf16),
@@ -197,6 +233,7 @@
             pltpu.VMEM((blocks - 1, step, hw + LANES), bf16),
             pltpu.VMEM((reps, step, hw + LANES), bf16),
             pltpu.VMEM((blocks, step, hw + LANES), bf16),
+            dma((8,)),
             dma((blocks,)), dma((blocks,)),
             dma((reps - 1,)), dma((reps - 1,)),
             dma((blocks - 1,)), dma((blocks - 1,)),
@@ -207,9 +244,20 @@
             collective_id=0, has_side_effects=True, vmem_limit_bytes=24 * 2**20
         ),
     )(
-        features, node_degree.reshape(1, quarter), edge_target, edge_source, edge_count,
-        layer_weight, layer_bias.reshape(1, hw), cotangent,
-    )
+        hbm(features), hbm(node_degree.reshape(1, quarter)), hbm(edge_target), hbm(edge_source),
+        hbm(edge_count), hbm(layer_weight), hbm(layer_bias.reshape(1, hw)), hbm(cotangent),
+    )
+    hidden, grad_weight, grad_bias = pl.pallas_call(
+        write_kernel,
+        out_shape=(
+            jax.ShapeDtypeStruct((quarter, hw), bf16),
+            jax.ShapeDtypeStruct((width, hw), jnp.float32),
+            jax.ShapeDtypeStruct((1, hw), jnp.float32),
+        ),
+        in_specs=[pl.BlockSpec(memory_space=pltpu.VMEM)] * 3,
+        out_specs=[pl.BlockSpec(memory_space=pltpu.HBM)] * 3,
+        scratch_shapes=[dma((3,))],
+    )(hidden, grad_weight, grad_bias)
     return hidden, grad_weight, grad_bias.reshape(hw)
 
 

time: 38 us -> 34.4 us (0.905)
  local copies, waits for them, and re-layouts: 7.17 us -> 1.88 us
  Pallas kernels: 29.8 us -> 31.7 us
    unnamed x19 -> x6, local copies, waits for them, and re-layouts: 7.17 us -> 1.88 us
    pallas_call x0 -> x1, Pallas kernels: none -> 1.69 us  [fused_per_device(): pl.pallas_call(write_kernel, out_shape=(jax.ShapeDtypeStruct((quarter, hw...]
where the time goes in v2:
time: 34.4 us; the launch traced here: 34.2 us
  Pallas kernels  31.7 us (92%)
  local copies, waits for them, and re-layouts  1.88 us (5%)
  between operations  0.65 us (2%)
    pallas_call x1, Pallas kernels, fused_per_device(): pl.pallas_call(layer_kernel, out_shape=(jax.ShapeDtypeStruct((quarter, hw...  30 us
    unnamed x6, local copies, waits for them, and re-layouts  1.88 us
    pallas_call x1, Pallas kernels, fused_per_device(): pl.pallas_call(write_kernel, out_shape=(jax.ShapeDtypeStruct((quarter, hw...  1.69 us

profile of v2, /device:TPU:0, one launch (start us, length us, event | category | flops | bytes accessed | tf_op | source)
XLA Modules:
  0.0 34.2 jit_solution(4517742391408986520)
XLA Ops:
  0.6 30.0 %shard_map.103 = (bf16[256,256]{1,0:T(8,128)(2,1)S(1)}, f32[128,256]{1,0:T(8,128)S(1)}, f32[1,256]{1,0:T(1,128)S(1)}) custom-call(bf16[256,128]{1,0:T(8,128)(2,1)} %feat_h.1, s32[1,256]{1,0:T(1,128)} %bitcast.3, s32[1,1,768]{2,1,0:T(1,128)} %tgt_h.1, s32[1,1,768]{2,1,0:T(1,128)} %src_h.1, s32[1,1,8]{2,1,0:T(1,128)} %cnt_h.1, bf16[128,256]{1,0:T(8,128)(2,1)} %w_h.1, ...), custom_call_target="tpu_custom_call" | custom-call | tf_op jit(solution)/shard_map/pallas_call | solution.py:208
  30.6 0.0 copy-start
  30.6 0.6 %copy-done = bf16[256,256]{1,0:T(8,128)(2,1)} copy-done((bf16[256,256]{1,0:T(8,128)(2,1)}, bf16[256,256]{1,0:T(8,128)(2,1)S(1)}, u32[]{:S(2)}) %copy-start) | copy-done | bytes 131096
  31.3 0.0 copy-start.1
  31.3 0.6 %copy-done.1 = f32[128,256]{1,0:T(8,128)} copy-done((f32[128,256]{1,0:T(8,128)}, f32[128,256]{1,0:T(8,128)S(1)}, u32[]{:S(2)}) %copy-start.1) | copy-done | bytes 131096
  31.9 0.0 copy-start.2
  31.9 0.6 %copy-done.2 = f32[1,256]{1,0:T(1,128)} copy-done((f32[1,256]{1,0:T(1,128)}, f32[1,256]{1,0:T(1,128)S(1)}, u32[]{:S(2)}) %copy-start.2) | copy-done | bytes 1048
  32.5 1.7 %shard_map.104 = (bf16[256,256]{1,0:T(8,128)(2,1)}, f32[128,256]{1,0:T(8,128)}, f32[1,256]{1,0:T(1,128)}) custom-call(bf16[256,256]{1,0:T(8,128)(2,1)} %copy-done, f32[128,256]{1,0:T(8,128)} %copy-done.1, f32[1,256]{1,0:T(1,128)} %copy-done.2), custom_call_target="tpu_custom_call" | custom-call | tf_op jit(solution)/shard_map/pallas_call | solution.py:250
Async XLA Ops:
  30.6 0.7 %copy-start = (bf16[256,256]{1,0:T(8,128)(2,1)}, bf16[256,256]{1,0:T(8,128)(2,1)S(1)}, u32[]{:S(2)}) copy-start(bf16[256,256]{1,0:T(8,128)(2,1)S(1)} %get-tuple-element.9.hid) | copy-start | bytes 393220
  31.3 0.6 %copy-start.1 = (f32[128,256]{1,0:T(8,128)}, f32[128,256]{1,0:T(8,128)S(1)}, u32[]{:S(2)}) copy-start(f32[128,256]{1,0:T(8,128)S(1)} %get-tuple-element.10.gw) | copy-start | bytes 393220
  31.9 0.6 %copy-start.2 = (f32[1,256]{1,0:T(1,128)}, f32[1,256]{1,0:T(1,128)S(1)}, u32[]{:S(2)}) copy-start(f32[1,256]{1,0:T(1,128)S(1)} %get-tuple-element.11.gb) | copy-start | bytes 3076

commit v3 on v2

--- a/solution.py
+++ b/solution.py
@@ -14,13 +14,14 @@
 def layer_kernel(
     feat_h, deg_h, tgt_h, src_h, cnt_h, w_h, bias_h, cot_h,
     hid, gw, gb,
-    feat, deg, tgt, src, cnt, w, bias, cot, ag, onehot, pick, gt, rs_out, rs_in, g_out, g_in, z_buf, f_buf,
-    in_s, ag_s, ag_r, rs_s, rs_r, g_s, g_r, z_s, z_r, f_s, f_r,
+    feat, deg, tgt, src, cnt, w, bias, cot, ag, onehot, pick, gt, rs_out, rs_in, c_out, c_in, a1, a2, b1, b2, f_out, f_in,
+    in_s, ag_s, ag_r, rs_s, rs_r, c_s, c_r, a1_s, a1_r, a2_s, a2_r, b1_s, b1_r, b2_s, b2_r, f_s, f_r,
 ):
     f32, bf16 = jnp.float32, jnp.bfloat16
     b, q = lax.axis_index("blk"), lax.axis_index("rep")
-    blocks, reps = ag.shape[0], z_buf.shape[0]
+    blocks, reps = ag.shape[1], onehot.shape[0]
     quarter, width = feat.shape
+    half = width // 2
     per_block = tgt.shape[-1] // blocks
     core, x, y = lax.rem(b, 2), lax.rem(lax.div(b, 2), 2), lax.div(b, 4)
 
@@ -51,7 +52,8 @@
         load.start()
 
     barrier = pltpu.get_barrier_semaphore()
-    for k in range(1, blocks):
+    near = (1, 2, 4, 6)
+    for k in near:
         pl.semaphore_signal(barrier, inc=1, device_id=(peer(k), q), device_id_type=MESH)
     for k in range(1, reps):
         pl.semaphore_signal(barrier, inc=1, device_id=(b, up(k)), device_id_type=MESH)
@@ -59,25 +61,22 @@
     loads[0].wait()
     loads[1].wait()
     inv_row = lax.rsqrt(deg[...].astype(f32))
-    ag[b] = (feat[...].astype(f32).T * inv_row).astype(bf16)
-
-    pl.semaphore_wait(barrier, blocks + reps - 2)
+    scaled = (feat[...].astype(f32).T * inv_row).astype(bf16)
+    for h in range(2):
+        ag[h, b] = scaled[h * half : (h + 1) * half]
+
+    pl.semaphore_wait(barrier, len(near) + reps - 1)
 
     sends = []
-    for k in (6, 2, 4, 1):
-        copy = push(ag.at[b], ag.at[b], ag_s.at[k], ag_r.at[b], peer(k), q)
-        copy.start()
-        sends.append(copy)
-
-    def arrived(k):
-        p = peer(k)
-        push(ag.at[p], ag.at[p], ag_s.at[k], ag_r.at[p], peer(k), q).wait_recv()
-
-    eye = lax.broadcasted_iota(jnp.int32, (quarter, quarter), 0) == lax.broadcasted_iota(
-        jnp.int32, (quarter, quarter), 1
-    )
-    inv = jnp.sum(jnp.where(eye, inv_row, 0.0), axis=1, keepdims=True)
-    scaled = (feat[...].astype(f32) * inv).astype(bf16).astype(f32)
+
+    def piece(h, k, p, to_b):
+        return push(ag.at[h, p], ag.at[h, p], ag_s.at[h, k], ag_r.at[h, p], to_b, q)
+
+    for h in range(2):
+        for k in (6, 2, 4, 1):
+            copy = piece(h, k, b, peer(k))
+            copy.start()
+            sends.append(copy)
 
     for load in loads[2:]:
         load.wait()
@@ -94,90 +93,120 @@
         for k in range(reps):
             onehot[k, :, here] = jnp.where(node + up(k) * quarter == t_c, 1.0, 0.0).astype(bf16)
 
-    for k in (2, 4, 6):
-        arrived(k)
-        p = peer(k)
-        copy = push(ag.at[p], ag.at[p], ag_s.at[k + 1], ag_r.at[p], peer(1), q)
-        copy.start()
-        sends.append(copy)
-    for k in (1, 3, 5, 7):
-        arrived(k)
-
-    for c in range(blocks):
-        rows = jnp.dot(ag[c], pick[c], preferred_element_type=f32)
-        gt[:, pl.ds(c * LANES, LANES)] = rows.astype(bf16)
-
-    own = None
-    for k in (2, 1, 3, 0):
-        part = lax.dot_general(
-            onehot[k], gt[...], (((1,), (1,)), ((), ())), preferred_element_type=f32
+    for h in range(2):
+        for k in (2, 4, 6):
+            piece(h, k, peer(k), peer(k)).wait_recv()
+            copy = piece(h, k + 1, peer(k), peer(1))
+            copy.start()
+            sends.append(copy)
+
+    def partial(h, k):
+        return push(
+            rs_out.at[h, k - 1], rs_in.at[h, k - 1], rs_s.at[h, k - 1], rs_r.at[h, k - 1], b, up(k)
         )
-        if k:
-            rs_out[k - 1] = part.astype(bf16)
-            copy = push(
-                rs_out.at[k - 1], rs_in.at[k - 1], rs_s.at[k - 1], rs_r.at[k - 1], b, up(k)
-            )
-            copy.start()
-            sends.append(copy)
-        else:
-            own = part + scaled
-    for k in (1, 3, 2):
-        push(
-            rs_out.at[k - 1], rs_in.at[k - 1], rs_s.at[k - 1], rs_r.at[k - 1], b, up(k)
-        ).wait_recv()
-        own = own + rs_in[k - 1].astype(f32)
-
-    agg = (own * inv).astype(bf16)
-    pre = jnp.dot(agg, w[...], preferred_element_type=f32) + bias[...]
+
+    def spread(h, k):
+        return lax.dot_general(
+            gt[h], onehot[k], (((1,), (1,)), ((), ())), preferred_element_type=f32
+        )
+
+    for h in range(2):
+        for k in (1, 3, 5, 7):
+            piece(h, k, peer(k), peer(k)).wait_recv()
+        for c in range(blocks):
+            rows = jnp.dot(ag[h, c], pick[c], preferred_element_type=f32)
+            gt[h, :, pl.ds(c * LANES, LANES)] = rows.astype(bf16)
+        for k in (2, 1, 3):
+            rs_out[h, k - 1] = spread(h, k).astype(bf16)
+            copy = partial(h, k)
+            copy.start()
+            sends.append(copy)
+    halves = []
+    for h in range(2):
+        own = spread(h, 0) + ag[h, b].astype(f32)
+        for k in (1, 3, 2):
+            partial(h, k).wait_recv()
+            own = own + rs_in[h, k - 1].astype(f32)
+        halves.append((own * inv_row).astype(bf16))
+    agg = jnp.concatenate(halves, axis=0)
+
+    pre = lax.dot_general(
+        agg, w[...], (((0,), (0,)), ((), ())), preferred_element_type=f32
+    ) + bias[...]
     sig = 1.0 / (1.0 + jnp.exp(-pre))
     grad = cot[...].astype(f32) * sig * (1.0 + pre * (1.0 - sig))
-    gwl = lax.dot_general(
-        agg, grad.astype(bf16), (((0,), (0,)), ((), ())), preferred_element_type=f32
-    )
+    gwl = jnp.dot(agg, grad.astype(bf16), preferred_element_type=f32)
     gbl = jnp.sum(grad, axis=0, keepdims=True)
-    step = width // blocks
     hw = gw.shape[1]
-    row = lax.broadcasted_iota(jnp.int32, (step, LANES), 0)
-    extra = jnp.where(row == 0, gbl[:, :LANES], jnp.where(row == 1, gbl[:, LANES:], 0.0))
-    for j in range(blocks):
-        g_out[j, :, :hw] = gwl[j * step : (j + 1) * step].astype(bf16)
-        g_out[j, :, hw:] = extra.astype(bf16)
-
-    def share(k):
-        return push(g_out.at[peer(k)], g_in.at[k - 1], g_s.at[k - 1], g_r.at[k - 1], peer(k), q)
-
-    for k in (6, 7, 2, 3, 4, 5, 1):
-        copy = share(k)
-        copy.start()
-        sends.append(copy)
+
+    chip, low = lax.div(b, 2), half // 2
+    first = core == 0
+    mine = jnp.where(first, gwl[:half], gwl[half:])
+    c_out[:half] = jnp.where(first, gwl[half:], gwl[:half]).astype(bf16)
+    c_out[half:] = jnp.broadcast_to(gbl, (c_out.shape[0] - half, hw)).astype(bf16)
+
+    def pair(k):
+        return push(c_out, c_in, c_s, c_r, peer(k), q)
+
+    copy = pair(1)
+    copy.start()
+    sends.append(copy)
     hid[...] = (pre * sig).astype(bf16)
-    part = g_out[b].astype(f32)
-    for k in (1, 2, 3, 4, 5, 6, 7):
-        share(k).wait_recv()
-        part = part + g_in[k - 1].astype(f32)
-    z_buf[q] = part.astype(bf16)
-    for k in (2, 1, 3):
-        copy = push(z_buf.at[q], z_buf.at[q], z_s.at[k], z_r.at[q], b, up(k))
-        copy.start()
-        sends.append(copy)
-    for k in (1, 3, 2):
-        p = up(k)
-        push(z_buf.at[p], z_buf.at[p], z_s.at[k], z_r.at[p], b, p).wait_recv()
-    part = z_buf[0].astype(f32)
-    for k in range(1, reps):
-        part = part + z_buf[k].astype(f32)
-    f_buf[b] = part.astype(bf16)
-    for k in (6, 7, 2, 3, 4, 5, 1):
-        copy = push(f_buf.at[b], f_buf.at[b], f_s.at[k], f_r.at[b], peer(k), q)
-        copy.start()
-        sends.append(copy)
-    for k in (1, 2, 3, 4, 5, 6, 7):
-        p = peer(k)
-        push(f_buf.at[p], f_buf.at[p], f_s.at[k], f_r.at[p], p, q).wait_recv()
-    for j in range(blocks):
-        gw[j * step : (j + 1) * step, :] = f_buf[j, :, :hw].astype(f32)
-    gb[:, :LANES] = f_buf[0, 0:1, hw : hw + LANES].astype(f32)
-    gb[:, LANES:] = f_buf[0, 1:2, hw : hw + LANES].astype(f32)
+
+    def over_plane(buf, sem_s, sem_r, k, p):
+        return push(buf.at[p], buf.at[p], sem_s.at[k // 2], sem_r.at[p], peer(k), q)
+
+    def over_rep(buf, sem_s, sem_r, k, p):
+        return push(buf.at[p], buf.at[p], sem_s.at[k], sem_r.at[p], b, up(k))
+
+    def send_plane(buf, sem_s, sem_r):
+        for k in (6, 2, 4):
+            copy = over_plane(buf, sem_s, sem_r, k, chip)
+            copy.start()
+            sends.append(copy)
+
+    def send_rep(buf, sem_s, sem_r):
+        for k in (3, 1, 2):
+            copy = over_rep(buf, sem_s, sem_r, k, q)
+            copy.start()
+            sends.append(copy)
+
+    def sum_plane(buf, sem_s, sem_r):
+        for k in (2, 4, 6):
+            over_plane(buf, sem_s, sem_r, k, lax.div(peer(k), 2)).wait_recv()
+        return sum(buf[p].astype(f32) for p in range(blocks // 2))
+
+    def sum_rep(buf, sem_s, sem_r):
+        for k in (1, 3, 2):
+            over_rep(buf, sem_s, sem_r, k, up(k)).wait_recv()
+        return sum(buf[p].astype(f32) for p in range(reps))
+
+    pair(1).wait_recv()
+    mine = mine + c_in[:half].astype(f32)
+    a1[chip, :low] = mine[:low].astype(bf16)
+    a1[chip, low:] = (c_out[half:].astype(f32) + c_in[half:].astype(f32)).astype(bf16)
+    b1[q] = mine[low:].astype(bf16)
+    send_rep(b1, b1_s, b1_r)
+    send_plane(a1, a1_s, a1_r)
+    a2[q] = sum_plane(a1, a1_s, a1_r).astype(bf16)
+    send_rep(a2, a2_s, a2_r)
+    b2[chip] = sum_rep(b1, b1_s, b1_r).astype(bf16)
+    send_plane(b2, b2_s, b2_r)
+    part_b = sum_plane(b2, b2_s, b2_r)
+    part_a = sum_rep(a2, a2_s, a2_r)
+    f_out[:low] = part_a[:low]
+    f_out[low:] = part_b
+
+    def swap(k):
+        return push(f_out, f_in, f_s, f_r, peer(k), q)
+
+    copy = swap(1)
+    copy.start()
+    sends.append(copy)
+    gb[...] = part_a[low : low + 1]
+    gw[pl.ds(pl.multiple_of(core * half, half), half), :] = f_out[...]
+    swap(1).wait_recv()
+    gw[pl.ds(pl.multiple_of((1 - core) * half, half), half), :] = f_in[...]
     for copy in sends:
         copy.wait_send()
 
@@ -199,7 +228,7 @@
     quarter, width = features.shape
     blocks, reps = lax.axis_size("blk"), lax.axis_size("rep")
     hw = layer_weight.shape[1]
-    step = width // blocks
+    half = width // 2
     bf16 = jnp.bfloat16
     dma = pltpu.SemaphoreType.DMA
     def hbm(array):
@@ -223,22 +252,29 @@
             pltpu.VMEM((width, hw), bf16),
             pltpu.VMEM((1, hw), jnp.float32),
             pltpu.VMEM((quarter, hw), bf16),
-            pltpu.VMEM((blocks, width, quarter), bf16),
+            pltpu.VMEM((2, blocks, width // 2, quarter), bf16),
             pltpu.VMEM((reps, quarter, blocks * LANES), bf16),
             pltpu.VMEM((blocks, quarter, LANES), bf16),
-            pltpu.VMEM((width, blocks * LANES), bf16),
-            pltpu.VMEM((reps - 1, quarter, width), bf16),
-            pltpu.VMEM((reps - 1, quarter, width), bf16),
-            pltpu.VMEM((blocks, step, hw + LANES), bf16),
-            pltpu.VMEM((blocks - 1, step, hw + LANES), bf16),
-            pltpu.VMEM((reps, step, hw + LANES), bf16),
-            pltpu.VMEM((blocks, step, hw + LANES), bf16),
+            pltpu.VMEM((2, width // 2, blocks * LANES), bf16),
+            pltpu.VMEM((2, reps - 1, width // 2, quarter), bf16),
+            pltpu.VMEM((2, reps - 1, width // 2, quarter), bf16),
+            pltpu.VMEM((half + 16, hw), bf16),
+            pltpu.VMEM((half + 16, hw), bf16),
+            pltpu.VMEM((blocks // 2, half // 2 + 16, hw), bf16),
+            pltpu.VMEM((reps, half // 2 + 16, hw), bf16),
+            pltpu.VMEM((reps, half // 2, hw), bf16),
+            pltpu.VMEM((blocks // 2, half // 2, hw), bf16),
+            pltpu.VMEM((half, hw), jnp.float32),
+            pltpu.VMEM((half, hw), jnp.float32),
             dma((8,)),
-            dma((blocks,)), dma((blocks,)),
-            dma((reps - 1,)), dma((reps - 1,)),
-            dma((blocks - 1,)), dma((blocks - 1,)),
+            dma((2, blocks)), dma((2, blocks)),
+            dma((2, reps - 1)), dma((2, reps - 1)),
+            dma, dma,
+            dma((blocks // 2,)), dma((blocks // 2,)),
             dma((reps,)), dma((reps,)),
-            dma((blocks,)), dma((blocks,)),
+            dma((reps,)), dma((reps,)),
+            dma((blocks // 2,)), dma((blocks // 2,)),
+            dma, dma,
         ],
         compiler_params=pltpu.CompilerParams(
             collective_id=0, has_side_effects=True, vmem_limit_bytes=24 * 2**20
@@ -257,6 +293,7 @@
         in_specs=[pl.BlockSpec(memory_space=pltpu.VMEM)] * 3,
         out_specs=[pl.BlockSpec(memory_space=pltpu.HBM)] * 3,
         scratch_shapes=[dma((3,))],
+        compiler_params=pltpu.CompilerParams(vmem_limit_bytes=2**20),
     )(hidden, grad_weight, grad_bias)
     return hidden, grad_weight, grad_bias.reshape(hw)
 

time: 34.4 us -> 30.9 us (0.90)
  local copies, waits for them, and re-layouts: 1.88 us -> 0 us
  Pallas kernels: 31.7 us -> 30.1 us
    unnamed x6 -> x0, local copies, waits for them, and re-layouts: 1.88 us -> none
    pallas_call x1, Pallas kernels: 1.69 us -> 0.73 us  [fused_per_device(): pl.pallas_call(write_kernel, out_shape=(jax.ShapeDtypeStruct((quarter, hw...]
    pallas_call x1, Pallas kernels: 30 us -> 29.4 us  [fused_per_device(): pl.pallas_call(layer_kernel, out_shape=(jax.ShapeDtypeStruct((quarter, hw...]
where the time goes in v3:
time: 30.9 us; the launch traced here: 30.8 us
  Pallas kernels  30.1 us (97%)
  between operations  0.64 us (2%)
    pallas_call x1, Pallas kernels, fused_per_device(): pl.pallas_call(layer_kernel, out_shape=(jax.ShapeDtypeStruct((quarter, hw...  29.4 us
    pallas_call x1, Pallas kernels, fused_per_device(): pl.pallas_call(write_kernel, out_shape=(jax.ShapeDtypeStruct((quarter, hw...  0.73 us

profile of v3, /device:TPU:0, one launch (start us, length us, event | category | flops | bytes accessed | tf_op | source)
XLA Modules:
  0.0 30.8 jit_solution(4510591698859460974)
XLA Ops:
  0.6 29.4 %shard_map.103 = (bf16[256,256]{1,0:T(8,128)(2,1)S(1)}, f32[128,256]{1,0:T(8,128)S(1)}, f32[1,256]{1,0:T(1,128)S(1)}) custom-call(bf16[256,128]{1,0:T(8,128)(2,1)} %feat_h.1, s32[1,256]{1,0:T(1,128)} %bitcast.3, s32[1,1,768]{2,1,0:T(1,128)} %tgt_h.1, s32[1,1,768]{2,1,0:T(1,128)} %src_h.1, s32[1,1,8]{2,1,0:T(1,128)} %cnt_h.1, bf16[128,256]{1,0:T(8,128)(2,1)} %w_h.1, ...), custom_call_target="tpu_custom_call" | custom-call | tf_op jit(solution)/shard_map/pallas_call | solution.py:237
  30.0 0.7 %shard_map.104 = (bf16[256,256]{1,0:T(8,128)(2,1)}, f32[128,256]{1,0:T(8,128)}, f32[1,256]{1,0:T(1,128)}) custom-call(bf16[256,256]{1,0:T(8,128)(2,1)S(1)} %get-tuple-element.9.hid, f32[128,256]{1,0:T(8,128)S(1)} %get-tuple-element.10.gw, f32[1,256]{1,0:T(1,128)S(1)} %get-tuple-element.11.gb), custom_call_target="tpu_custom_call" | custom-call | tf_op jit(solution)/shard_map/pallas_call | solution.py:286

commit v4 on v3

--- a/solution.py
+++ b/solution.py
@@ -73,14 +73,19 @@
         return push(ag.at[h, p], ag.at[h, p], ag_s.at[h, k], ag_r.at[h, p], to_b, q)
 
     for h in range(2):
-        for k in (6, 2, 4, 1):
+        for k in (6, 2, 4):
             copy = piece(h, k, b, peer(k))
             copy.start()
             sends.append(copy)
+    for h in range(2):
+        copy = piece(h, 1, b, peer(1))
+        copy.start()
+        sends.append(copy)
 
     for load in loads[2:]:
         load.wait()
     node = lax.broadcasted_iota(jnp.int32, (quarter, LANES), 0)
+    target = lax.broadcasted_iota(jnp.int32, (LANES, quarter), 1)
     lane = lax.broadcasted_iota(jnp.int32, (1, LANES), 1)
     fill = jnp.full((1, LANES - per_block), -1, jnp.int32)
     for c in range(blocks):
@@ -89,9 +94,11 @@
         s_c = jnp.concatenate([src[0, :, c * per_block : (c + 1) * per_block], fill], axis=1)
         t_c = jnp.concatenate([tgt[0, :, c * per_block : (c + 1) * per_block], fill], axis=1)
         t_c = jnp.where(live, t_c, -1)
+        column = jnp.broadcast_to(t_c.astype(f32), (LANES, LANES)).T.astype(jnp.int32)
+        column = jnp.concatenate([column] * (quarter // LANES), axis=1)
         pick[c] = jnp.where(node == s_c, 1.0, 0.0).astype(bf16)
         for k in range(reps):
-            onehot[k, :, here] = jnp.where(node + up(k) * quarter == t_c, 1.0, 0.0).astype(bf16)
+            onehot[k, here] = jnp.where(column - up(k) * quarter == target, 1.0, 0.0).astype(bf16)
 
     for h in range(2):
         for k in (2, 4, 6):
@@ -106,9 +113,7 @@
         )
 
     def spread(h, k):
-        return lax.dot_general(
-            gt[h], onehot[k], (((1,), (1,)), ((), ())), preferred_element_type=f32
-        )
+        return jnp.dot(gt[h], onehot[k], preferred_element_type=f32)
 
     for h in range(2):
         for k in (1, 3, 5, 7):
@@ -253,7 +258,7 @@
             pltpu.VMEM((1, hw), jnp.float32),
             pltpu.VMEM((quarter, hw), bf16),
             pltpu.VMEM((2, blocks, width // 2, quarter), bf16),
-            pltpu.VMEM((reps, quarter, blocks * LANES), bf16),
+            pltpu.VMEM((reps, blocks * LANES, quarter), bf16),
             pltpu.VMEM((blocks, quarter, LANES), bf16),
             pltpu.VMEM((2, width // 2, blocks * LANES), bf16),
             pltpu.VMEM((2, reps - 1, width // 2, quarter), bf16),

time: 30.9 us -> 30.8 us (level)
  no operation moved by 1% of the time
where the time goes in v4:
time: 30.8 us; the launch traced here: 30.7 us
  Pallas kernels  30 us (97%)
  between operations  0.64 us (2%)
    pallas_call x1, Pallas kernels, fused_per_device(): pl.pallas_call(layer_kernel, out_shape=(jax.ShapeDtypeStruct((quarter, hw...  29.3 us
    pallas_call x1, Pallas kernels, fused_per_device(): pl.pallas_call(write_kernel, out_shape=(jax.ShapeDtypeStruct((quarter, hw...  0.73 us

profile of v4, /device:TPU:0, one launch (start us, length us, event | category | flops | bytes accessed | tf_op | source)
XLA Modules:
  0.0 30.7 jit_solution(7027257145043780234)
XLA Ops:
  0.6 29.3 %shard_map.103 = (bf16[256,256]{1,0:T(8,128)(2,1)S(1)}, f32[128,256]{1,0:T(8,128)S(1)}, f32[1,256]{1,0:T(1,128)S(1)}) custom-call(bf16[256,128]{1,0:T(8,128)(2,1)} %feat_h.1, s32[1,256]{1,0:T(1,128)} %bitcast.3, s32[1,1,768]{2,1,0:T(1,128)} %tgt_h.1, s32[1,1,768]{2,1,0:T(1,128)} %src_h.1, s32[1,1,8]{2,1,0:T(1,128)} %cnt_h.1, bf16[128,256]{1,0:T(8,128)(2,1)} %w_h.1, ...), custom_call_target="tpu_custom_call" | custom-call | tf_op jit(solution)/shard_map/pallas_call | solution.py:242
  29.9 0.7 %shard_map.104 = (bf16[256,256]{1,0:T(8,128)(2,1)}, f32[128,256]{1,0:T(8,128)}, f32[1,256]{1,0:T(1,128)}) custom-call(bf16[256,256]{1,0:T(8,128)(2,1)S(1)} %get-tuple-element.9.hid, f32[128,256]{1,0:T(8,128)S(1)} %get-tuple-element.10.gw, f32[1,256]{1,0:T(1,128)S(1)} %get-tuple-element.11.gb), custom_call_target="tpu_custom_call" | custom-call | tf_op jit(solution)/shard_map/pallas_call | solution.py:291
